TPU v7x, 256 devices: a whole 4x4x8 slice. The times are simulated.
256 devices in a mesh: gx: 8 (over z), gy: 4 (over x_lo, core), gz: 8 (over y, x_hi).
Axes of the slice: x: 4 (x_hi: 2, x_lo: 2; x = x_hi * 2 + x_lo), y: 4, z: 8, core: 2. Of those that a mesh axis runs over, the one named last changes fastest.
Arguments:
- tokens: bfloat16 [2048, 6144], P(('gy', 'gx'), 'gz'), may hold values from -6 to 6
- w_in: bfloat16 [6144, 24576], P('gz', ('gx', 'gy')), may hold values from -0.078125 to 0.078125
- w_out: bfloat16 [24576, 6144], P(('gx', 'gy'), 'gz')
- out_grad: bfloat16 [2048, 6144], P(('gy', 'gx'), 'gz')
Outputs:
- in_grad: bfloat16 [2048, 6144], P(('gy', 'gx'), 'gz')
- grad_in_clipped: bfloat16 [6144, 24576], P('gz', ('gx', 'gy'))
- grad_out_clipped: bfloat16 [24576, 6144], P(('gx', 'gy'), 'gz')
All inputs are finite; a program needn't handle non-finite values.
Results may differ from a plain program's by a relative error of at most 0.025.
Values may be sent and summed in bfloat16 or wider, within the bound.
A program may use at most 128 MiB of HBM per device.

v0:
```python
import jax
import jax.numpy as jnp
from jax import lax
from jax.sharding import PartitionSpec as P

D = 6144
FW = 24576


GELU_C = 0.7978845608


def gelu_parts(values):
    inner_arg = GELU_C * (values + 0.044715 * values * values * values)
    tanh_val = jnp.tanh(inner_arg)
    value_out = 0.5 * values * (1.0 + tanh_val)
    slope = 0.5 * (1.0 + tanh_val) + 0.5 * values * (1.0 - tanh_val * tanh_val) * GELU_C * (
        1.0 + 3.0 * 0.044715 * values * values
    )
    return (value_out, slope)


def contract(left, right, left_dim, right_dim):
    return lax.dot_general(
        left, right, (((left_dim,), (right_dim,)), ((), ())), preferred_element_type=jnp.float32
    )


def shards(tokens, w_in, w_out, out_grad):
    x_blk, dy_blk = (
        lax.all_gather(tokens, "gx", axis=0, tiled=True),
        lax.all_gather(out_grad, "gx", axis=0, tiled=True),
    )
    w_in_full, w_out_full = (
        lax.all_gather(w_in, "gy", axis=1, tiled=True),
        lax.all_gather(w_out, "gy", axis=0, tiled=True),
    )
    h_term = contract(x_blk, w_in_full, 1, 0)
    d_term = contract(dy_blk, w_out_full, 1, 1)
    pre_act, d_act = (
        lax.psum_scatter(h_term.astype(jnp.bfloat16), "gz", scatter_dimension=0, tiled=True).astype(
            jnp.float32
        ),
        lax.psum_scatter(d_term.astype(jnp.bfloat16), "gz", scatter_dimension=0, tiled=True).astype(
            jnp.float32
        ),
    )
    value_out, slope = gelu_parts(pre_act)
    act_rows = value_out.astype(jnp.bfloat16)
    d_pre = (d_act * slope).astype(jnp.bfloat16)
    act_full, d_pre_full = (
        lax.all_gather(act_rows, "gz", axis=0, tiled=True),
        lax.all_gather(d_pre, "gz", axis=0, tiled=True),
    )
    dx_term = contract(d_pre_full, w_in_full, 1, 1)
    in_grad = lax.psum_scatter(dx_term.astype(jnp.bfloat16), "gx", scatter_dimension=0, tiled=True)
    gin_term = contract(x_blk, d_pre_full, 0, 0)
    gout_term = contract(act_full, dy_blk, 0, 0)
    grad_in, grad_out = (
        lax.psum_scatter(
            gin_term.astype(jnp.bfloat16), "gy", scatter_dimension=1, tiled=True
        ).astype(jnp.float32),
        lax.psum_scatter(
            gout_term.astype(jnp.bfloat16), "gy", scatter_dimension=0, tiled=True
        ).astype(jnp.float32),
    )
    local_square = jnp.sum(grad_in * grad_in) + jnp.sum(grad_out * grad_out)
    grand_total = lax.psum(local_square, ("gx", "gy", "gz"))
    factor = 1.0 / jnp.sqrt(grand_total / (2.0 * D * FW) + 1e-06)
    return (
        in_grad,
        (grad_in * factor).astype(jnp.bfloat16),
        (grad_out * factor).astype(jnp.bfloat16),
    )


def solution(mesh):
    placed = (
        P(("gy", "gx"), "gz"),
        P("gz", ("gx", "gy")),
        P(("gx", "gy"), "gz"),
        P(("gy", "gx"), "gz"),
    )
    return jax.shard_map(
        shards,
        mesh=mesh,
        in_specs=placed,
        out_specs=(P(("gy", "gx"), "gz"), P("gz", ("gx", "gy")), P(("gx", "gy"), "gz")),
        check_vma=False,
    )
```

profile of v0, /device:TPU:1, one launch (start us, length us, event | category | flops | bytes accessed | tf_op | source)
XLA Modules:
  0.0 639.9 jit_solution(16579842333017380937)
XLA Ops:
  7.2 0.0 all-gather.5.cloned.1.call-start
  7.2 0.7 all-gather.5.cloned.1.call-update
  7.9 0.0 all-gather.7.cloned.1.call-start
  7.9 0.7 all-gather.7.cloned.1.call-update
  8.6 0.0 reduce-scatter.6.cloned.1.call-start
  8.7 24.8 %all_gather.18 = bf16[512,768]{1,0:T(8,128)(2,1)S(1)} all-gather(bf16[64,768]{1,0:T(8,128)(2,1)} %param.7), channel_id=1, replica_groups=mesh['gx'=8,'gy'=4,'gz'=8] {'gx'}, dimensions={0}, use_global_device_ids=true | all-gather | bytes 884736 | tf_op jit(solution)/shard_map/all_gather | solution.py:32
  33.5 34.0 %all-gather.5.cloned.1.call-done = bf16[3072,768]{1,0:T(8,128)(2,1)} async-done(((bf16[768,768]{1,0:T(8,128)(2,1)}), bf16[3072,768]{1,0:T(8,128)(2,1)}) %all-gather.5.cloned.1.call-update) | async-done | bytes 4718608 | tf_op jit(solution)/shard_map/all_gather | solution.py:36
  67.5 6.3 convolution_convert_fusion.3
  73.8 0.0 copy-start.1
  73.8 0.0 reduce-scatter.6.cloned.1.call-update
  73.9 0.0 reduce-scatter.8.cloned.1.call-start
  73.9 0.8 copy-done.1
  74.7 23.3 %all_gather.20 = bf16[512,768]{1,0:T(8,128)(2,1)S(1)} all-gather(bf16[64,768]{1,0:T(8,128)(2,1)S(1)} %copy-done.1), channel_id=1, replica_groups=mesh['gx'=8,'gy'=4,'gz'=8] {'gx'}, dimensions={0}, use_global_device_ids=true | all-gather | bytes 884736 | tf_op jit(solution)/shard_map/all_gather | solution.py:31
  98.0 25.7 %all-gather.7.cloned.1.call-done = bf16[768,3072]{1,0:T(8,128)(2,1)} async-done(((bf16[768,768]{1,0:T(8,128)(2,1)}), bf16[768,3072]{1,0:T(8,128)(2,1)}) %all-gather.7.cloned.1.call-update) | async-done | bytes 4718608 | tf_op jit(solution)/shard_map/all_gather | solution.py:35
  123.7 6.3 convolution_convert_fusion.2
  129.9 0.0 reduce-scatter.8.cloned.1.call-update
  130.0 0.0 all-gather.9.cloned.1.call-start
  130.0 81.4 %reduce-scatter.6.cloned.1.call-done = bf16[64,3072]{1,0:T(8,128)(2,1)} async-done(((bf16[512,3072]{1,0:T(8,128)(2,1)}), bf16[64,3072]{1,0:T(8,128)(2,1)}) %reduce-scatter.6.cloned.1.call-update) | async-done | bytes 393232 | tf_op jit(solution)/shard_map/reduce_scatter | solution.py:44
  211.4 87.2 %reduce-scatter.8.cloned.1.call-done = bf16[64,3072]{1,0:T(8,128)(2,1)} async-done(((bf16[512,3072]{1,0:T(8,128)(2,1)}), bf16[64,3072]{1,0:T(8,128)(2,1)}) %reduce-scatter.8.cloned.1.call-update) | async-done | bytes 393232 | tf_op jit(solution)/shard_map/reduce_scatter | solution.py:41
  298.7 2.6 fusion.12
  301.2 0.0 all-gather.9.cloned.1.call-update
  301.3 0.0 all-gather.11.cloned.1.call-start
  301.3 0.5 all-gather.11.cloned.1.call-update
  301.9 0.0 reduce-scatter.12.cloned.1.call-start
  301.9 67.2 %all-gather.9.cloned.1.call-done = bf16[512,3072]{1,0:T(8,128)(2,1)} async-done(((bf16[64,3072]{1,0:T(8,128)(2,1)}), bf16[512,3072]{1,0:T(8,128)(2,1)}) %all-gather.9.cloned.1.call-update) | async-done | bytes 3145744 | tf_op jit(solution)/shard_map/all_gather | solution.py:53
  369.1 6.7 %fusion = bf16[768,3072]{0,1:T(8,128)(2,1)} fusion(bf16[512,3072]{1,0:T(8,128)(2,1)} %all-gather.9.cloned.1.call-done, bf16[512,768]{1,0:T(8,128)(2,1)S(1)} %all_gather.20), kind=kOutput, calls=%fused_computation.2 | convolution fusion | flops 2418278400 | bytes 8650752 | tf_op jit(solution)/shard_map/dot_general | solution.py:24
  375.9 0.0 reduce-scatter.12.cloned.1.call-update
  375.9 0.0 reduce-scatter.14.cloned.1.call-start
  375.9 61.9 %all-gather.11.cloned.1.call-done = bf16[512,3072]{1,0:T(8,128)(2,1)} async-done(((bf16[64,3072]{1,0:T(8,128)(2,1)}), bf16[512,3072]{1,0:T(8,128)(2,1)}) %all-gather.11.cloned.1.call-update) | async-done | bytes 3145744 | tf_op jit(solution)/shard_map/all_gather | solution.py:52
  437.8 6.3 convolution_convert_fusion
  444.1 0.0 copy-start.2
  444.1 0.0 reduce-scatter.14.cloned.1.call-update
  444.1 0.0 reduce-scatter.10.cloned.1.call-start
  444.1 1.8 copy-done.2
  446.0 5.9 convolution_convert_fusion.4
  451.8 0.0 reduce-scatter.10.cloned.1.call-update
  451.9 39.3 %reduce-scatter.12.cloned.1.call-done = bf16[768,768]{0,1:T(8,128)(2,1)} async-done(((bf16[768,3072]{0,1:T(8,128)(2,1)}), bf16[768,768]{0,1:T(8,128)(2,1)}) %reduce-scatter.12.cloned.1.call-update) | async-done | bytes 1179664 | tf_op jit(solution)/shard_map/reduce_scatter | solution.py:60
  491.2 0.0 copy-start
  491.2 2.6 fusion.1
  493.8 53.2 %reduce-scatter.14.cloned.1.call-done = bf16[768,768]{0,1:T(8,128)(2,1)} async-done(((bf16[3072,768]{0,1:T(8,128)(2,1)}), bf16[768,768]{0,1:T(8,128)(2,1)}) %reduce-scatter.14.cloned.1.call-update) | async-done | bytes 1179664 | tf_op jit(solution)/shard_map/reduce_scatter | solution.py:63
  546.9 2.5 fusion.3
  550.7 77.4 %psum.7 = f32[]{:T(128)} all-reduce(f32[]{:T(128)S(6)} %add.35), channel_id=1, replica_groups=mesh['gx'=8,'gy'=4,'gz'=8] {'gx','gy','gz'}, use_global_device_ids=true, to_apply=%region_7.0 | all-reduce | flops 1 | bytes 8 | tf_op jit(solution)/shard_map/psum | solution.py:68
  628.8 0.0 copy-done
  628.8 1.7 fusion.2
  630.5 1.5 copy.8
  631.9 1.4 copy.9
  633.4 0.0 reduce-scatter.10.cloned.1.call-done
Async XLA Ops:
  7.2 60.3 %all-gather.5.cloned.1.call-start = ((), (), s32[]{:S(2)}) async-start(), calls=%async_computation.5 | async-start | bytes 5898240 | tf_op jit(solution)/shard_map/all_gather | solution.py:36
  7.9 115.8 %all-gather.7.cloned.1.call-start = ((), (), s32[]{:S(2)}) async-start(), calls=%async_computation.7 | async-start | bytes 5898240 | tf_op jit(solution)/shard_map/all_gather | solution.py:35
  8.6 202.8 %reduce-scatter.6.cloned.1.call-start = ((), (), s32[]{:S(2)}) async-start(), calls=%async_computation.6 | async-start | bytes 3538944 | tf_op jit(solution)/shard_map/reduce_scatter | solution.py:44
  73.8 0.9 copy-start.1
  73.9 224.8 %reduce-scatter.8.cloned.1.call-start = ((), (), s32[]{:S(2)}) async-start(), calls=%async_computation.8 | async-start | bytes 3538944 | tf_op jit(solution)/shard_map/reduce_scatter | solution.py:41
  130.0 239.2 %all-gather.9.cloned.1.call-start = ((), (), s32[]{:S(2)}) async-start(), calls=%async_computation.9 | async-start | bytes 3538944 | tf_op jit(solution)/shard_map/all_gather | solution.py:53
  301.3 136.5 %all-gather.11.cloned.1.call-start = ((), (), s32[]{:S(2)}) async-start(), calls=%async_computation.12 | async-start | bytes 3538944 | tf_op jit(solution)/shard_map/all_gather | solution.py:52
  301.9 189.3 %reduce-scatter.12.cloned.1.call-start = ((), (), s32[]{:S(2)}) async-start(), calls=%async_computation.11 | async-start | bytes 5898240 | tf_op jit(solution)/shard_map/reduce_scatter | solution.py:60
  375.9 171.0 %reduce-scatter.14.cloned.1.call-start = ((), (), s32[]{:S(2)}) async-start(), calls=%async_computation.13 | async-start | bytes 5898240 | tf_op jit(solution)/shard_map/reduce_scatter | solution.py:63
  444.1 1.9 copy-start.2
  444.1 189.3 %reduce-scatter.10.cloned.1.call-start = ((), (), s32[]{:S(2)}) async-start(), calls=%async_computation.10 | async-start | bytes 884736 | tf_op jit(solution)/shard_map/reduce_scatter | solution.py:56
  491.2 137.6 %copy-start = (bf16[768,768]{0,1:T(8,128)(2,1)S(1)}, bf16[768,768]{0,1:T(8,128)(2,1)}, u32[]{:S(2)}) copy-start(bf16[768,768]{0,1:T(8,128)(2,1)} %reduce-scatter.12.cloned.1.call-done) | copy-start | bytes 3538948
Sparse Core Ops, SparseCore 0:
  9.8 57.6 all-gather.4
  69.3 54.3 all-gather.6
  127.8 83.5 reduce-scatter.5
  215.4 83.1 reduce-scatter.7
  301.7 67.3 all-gather.8
  372.1 65.6 all-gather.10
  440.4 50.7 reduce-scatter.11
  493.7 53.1 reduce-scatter.13
  550.0 34.1 reduce-scatter.9
where the time goes:
time: 640 us
  waiting for transfers between devices  452 us (71%)
  blocking collectives  125 us (20%)
  matrix products  31.5 us (5%)
  between operations  15.9 us (2%)
  other arithmetic  9.35 us (1%)
    reduce_scatter x1, waiting for transfers between devices, shards(): lax.psum_scatter(h_term.astype(jnp.bfloat16), 'gz', scatter_dimension=0,...  87.2 us
    reduce_scatter x1, waiting for transfers between devices, shards(): lax.psum_scatter(d_term.astype(jnp.bfloat16), 'gz', scatter_dimension=0,...  81.4 us
    psum x1, blocking collectives, shards(): grand_total = lax.psum(local_square, ('gx', 'gy', 'gz'))  77.4 us
    all_gather x1, waiting for transfers between devices, shards(): lax.all_gather(d_pre, 'gz', axis=0, tiled=True)  67.2 us
    all_gather x1, waiting for transfers between devices, shards(): lax.all_gather(act_rows, 'gz', axis=0, tiled=True)  61.9 us
    reduce_scatter x1, waiting for transfers between devices, shards(): lax.psum_scatter(gout_term.astype(jnp.bfloat16), 'gy', scatter_dimension=...  53.2 us
    reduce_scatter x1, waiting for transfers between devices, shards(): lax.psum_scatter(gin_term.astype(jnp.bfloat16), 'gy', scatter_dimension=1...  39.3 us
    all_gather x1, waiting for transfers between devices, shards(): lax.all_gather(w_out, 'gy', axis=0, tiled=True)  34 us
  transfers between devices with their start and end apart: 9, of which 8 were waited for; matrix products, arithmetic and copies ran while one was open for 6% of the time, Pallas kernels for 0%

commit v1 on v0

v1 whole, which is shorter than its diff:
```python
import jax
import jax.numpy as jnp
from jax import lax
from jax.experimental import pallas as pl
from jax.experimental.pallas import tpu as pltpu
from jax.sharding import PartitionSpec as P

D = 6144
FW = 24576
GELU_C = 0.7978845608
MESH = pl.DeviceIdType.MESH

NB = 8
ROWS = 128
HALF = 64
W = 768
Q = 384
F32 = jnp.float32
BF16 = jnp.bfloat16


def gelu_parts(values):
    square = values * values
    inner_arg = GELU_C * (values + 0.044715 * square * values)
    tanh_val = jnp.tanh(inner_arg)
    value_out = 0.5 * values * (1.0 + tanh_val)
    slope = 0.5 * (1.0 + tanh_val) + 0.5 * values * (1.0 - tanh_val * tanh_val) * GELU_C * (
        1.0 + 3.0 * 0.044715 * square
    )
    return (value_out, slope)


def contract(left, right, left_dim, right_dim):
    return lax.dot_general(
        left, right, (((left_dim,), (right_dim,)), ((), ())), preferred_element_type=F32
    )


def kernel(
    tok, win, wout, dy, o_dx, o_gin, o_gout,
    xall, wsib, part, got, xgot, full, acc_in, acc_out, dxs, dxr, gs_in, gs_out, gr_in, gr_out,
    sq, sqr1, sqr2,
    ss, rs, wss, wrs, gss, grs, s1s, s1r, s2s, s2r,
):
    z, gy, gz = lax.axis_index("gx"), lax.axis_index("gy"), lax.axis_index("gz")
    yy, xh = gz // 2, gz % 2
    xl, core = gy // 2, gy % 2
    up, down, far = (yy + 1) % 4, (yy + 3) % 4, (yy + 2) % 4
    to_up, to_down = {"gz": up * 2 + xh}, {"gz": down * 2 + xh}
    to_hi = {"gz": yy * 2 + 1 - xh}
    other_gy = (1 - xl) * 2 + core
    to_lo = {"gy": other_gy}
    to_sib = {"gy": xl * 2 + 1 - core}

    group_one = [
        (dz * 2 + k, {"gx": (z + dz) % 8, "gy": other_gy if k else gy})
        for dz in range(8) for k in range(2) if dz + k
    ]
    group_two = [
        (d * 4 + kx * 2 + kc, {
            "gz": ((yy + d) % 4) * 2 + (1 - xh if kx else xh),
            "gy": xl * 2 + (1 - core if kc else core),
        })
        for d in range(4) for kx in range(2) for kc in range(2) if d + kx + kc
    ]

    def put(src, dst, send, recv, where):
        pltpu.make_async_remote_copy(
            src_ref=src, dst_ref=dst, send_sem=send, recv_sem=recv,
            device_id=where, device_id_type=MESH,
        ).start()

    def arrived(ref, sem):
        pltpu.make_async_remote_copy(
            src_ref=ref, dst_ref=ref, send_sem=sem, recv_sem=sem,
            device_id=to_up, device_id_type=MESH,
        ).wait_recv()

    def left(ref, sem):
        pltpu.make_async_remote_copy(
            src_ref=ref, dst_ref=ref, send_sem=sem, recv_sem=sem,
            device_id=to_up, device_id_type=MESH,
        ).wait_send()

    barrier = pltpu.get_barrier_semaphore()
    for _, where in group_one + group_two:
        pl.semaphore_signal(barrier, inc=1, device_id=where, device_id_type=MESH)
    pl.semaphore_wait(barrier, 30)

    xall[0, 0, 0:HALF] = tok[...]
    xall[0, 1, 0:HALF] = dy[...]
    put(xall.at[0, :, 0:HALF], xall.at[0, :, HALF:ROWS], ss.at[0, 13], rs.at[0, 13], to_lo)
    put(win, wsib.at[0], wss.at[0], wrs.at[0], to_sib)
    put(wout, wsib.at[1], wss.at[1], wrs.at[1], to_sib)

    acc_in[...] = jnp.zeros_like(acc_in)
    acc_out[...] = jnp.zeros_like(acc_out)

    def products(b):
        @pl.when(b == 0)
        def _():
            arrived(xall.at[0, :, HALF:ROWS], rs.at[0, 13])
            put(xall.at[0], xall.at[1], ss.at[1, 13], rs.at[1, 13], {"gx": (z + 1) % 8})
            put(xall.at[0], xall.at[2], ss.at[2, 13], rs.at[2, 13], {"gx": (z + 7) % 8})

        @pl.when(b > 0)
        def _():
            arrived(xall.at[b], rs.at[b, 13])

        @pl.when((b > 0) & (b < NB - 2))
        def _():
            nxt = (z + 7 + 2 * (b % 2)) % 8
            put(xall.at[b], xall.at[b + 2], ss.at[b + 2, 13], rs.at[b + 2, 13], {"gx": nxt})

        def one(which, w_in, w_out):
            h = contract(xall[b, 0], w_in, 1, 0).astype(BF16)
            part[b, 2 * which, 0] = h[:, :Q]
            part[b, 2 * which + 1, 0] = h[:, Q:]
            d = contract(xall[b, 1], w_out, 1, 1).astype(BF16)
            part[b, 2 * which, 1] = d[:, :Q]
            part[b, 2 * which + 1, 1] = d[:, Q:]

        one(0, win[...], wout[...])

        @pl.when(b == 0)
        def _():
            arrived(wsib.at[0], wrs.at[0])
            arrived(wsib.at[1], wrs.at[1])

        one(1, wsib[0], wsib[1])
        put(part.at[b, far, 0], got.at[b, 0], ss.at[b, 0], rs.at[b, 0], to_up)
        put(part.at[b, far, 1], got.at[b, 2], ss.at[b, 2], rs.at[b, 2], to_down)
        put(part.at[b, up, 1], got.at[b, 1], ss.at[b, 1], rs.at[b, 1], to_up)
        put(part.at[b, down, 0], got.at[b, 3], ss.at[b, 3], rs.at[b, 3], to_down)

    def relay_sums(b):
        arrived(got.at[b, 0], rs.at[b, 0])
        part[b, up, 0] = (part[b, up, 0].astype(F32) + got[b, 0].astype(F32)).astype(BF16)
        put(part.at[b, up, 0], got.at[b, 4], ss.at[b, 4], rs.at[b, 4], to_up)
        arrived(got.at[b, 2], rs.at[b, 2])
        part[b, down, 1] = (part[b, down, 1].astype(F32) + got[b, 2].astype(F32)).astype(BF16)
        put(part.at[b, down, 1], got.at[b, 5], ss.at[b, 5], rs.at[b, 5], to_down)

    def quarter_sums(b):
        for k in (1, 3, 4, 5):
            arrived(got.at[b, k], rs.at[b, k])
        part[b, yy, 0] = (
            part[b, yy, 0].astype(F32) + got[b, 3].astype(F32) + got[b, 4].astype(F32)
        ).astype(BF16)
        part[b, yy, 1] = (
            part[b, yy, 1].astype(F32) + got[b, 1].astype(F32) + got[b, 5].astype(F32)
        ).astype(BF16)
        put(part.at[b, yy], xgot.at[b], ss.at[b, 6], rs.at[b, 6], to_hi)

    def activate(b):
        arrived(xgot.at[b], rs.at[b, 6])
        value_out, slope = gelu_parts(part[b, yy, 0].astype(F32) + xgot[b, 0].astype(F32))
        full[b, yy, 0] = value_out.astype(BF16)
        full[b, yy, 1] = (
            (part[b, yy, 1].astype(F32) + xgot[b, 1].astype(F32)) * slope
        ).astype(BF16)
        put(full.at[b, yy], full.at[b, yy], ss.at[b, 7], rs.at[b, 7], to_up)
        put(full.at[b, yy], full.at[b, yy], ss.at[b, 8], rs.at[b, 8], to_down)

    def relay_acts(b):
        arrived(full.at[b, down], rs.at[b, 7])
        put(full.at[b, down, 0], full.at[b, down, 0], ss.at[b, 9], rs.at[b, 9], to_up)
        arrived(full.at[b, up], rs.at[b, 8])
        put(full.at[b, up, 1], full.at[b, up, 1], ss.at[b, 10], rs.at[b, 10], to_down)

    def input_grad(b):
        arrived(full.at[b, far, 0], rs.at[b, 9])
        arrived(full.at[b, far, 1], rs.at[b, 10])
        own = jnp.concatenate([full[b, 0, 1], full[b, 1, 1]], axis=1)
        sib = jnp.concatenate([full[b, 2, 1], full[b, 3, 1]], axis=1)
        dxs[b] = (contract(own, win[...], 1, 1) + contract(sib, wsib[0], 1, 1)).astype(BF16)
        owner = (z + 8 + (b // 2) * (1 - b % 2) - ((b + 1) // 2) * (b % 2)) % 8

        @pl.when(b > 0)
        def _():
            put(dxs.at[b, 0:HALF], dxr.at[b, 0], ss.at[b, 11], rs.at[b, 11], {"gx": owner})

        put(
            dxs.at[b, HALF:ROWS], dxr.at[b, 1], ss.at[b, 12], rs.at[b, 12],
            {"gx": owner, "gy": other_gy},
        )

    def weight_grads(b):
        first = b - 1
        x_t = jnp.concatenate([xall[first, 0], xall[b, 0]], axis=0).T
        dy_pair = jnp.concatenate([xall[first, 1], xall[b, 1]], axis=0)

        @pl.loop(0, 4)
        def _(q):
            act_t = jnp.concatenate([full[first, q, 0], full[b, q, 0]], axis=0).T
            d_pre = jnp.concatenate([full[first, q, 1], full[b, q, 1]], axis=0)
            acc_in[q] += contract(x_t, d_pre, 1, 0)
            acc_out[q] += contract(act_t, dy_pair, 1, 0)

    stages = (products, relay_sums, quarter_sums, activate, relay_acts, input_grad)

    @pl.loop(0, NB + len(stages) - 1)
    def _(t):
        for lag, stage in enumerate(stages):
            b = t - lag

            @pl.when((b >= 0) & (b < NB))
            def _(stage=stage, b=b):
                stage(b)

        last = t - (len(stages) - 1)

        @pl.when((last >= 0) & (last % 2 == 1))
        def _():
            weight_grads(last)

    for j in range(2):
        gs_in[j] = acc_in[2 + j].astype(BF16)
        put(gs_in.at[j], gr_in.at[j], gss.at[j], grs.at[j], to_sib)
        gs_out[j] = acc_out[2 + j].astype(BF16)
        put(gs_out.at[j], gr_out.at[j], gss.at[2 + j], grs.at[2 + j], to_sib)

    total = dxs[0, 0:HALF].astype(F32)
    for b in range(NB):
        for k in range(2):
            if b + k:
                arrived(dxr.at[b, k], rs.at[b, 11 + k])
                total += dxr[b, k].astype(F32)
    o_dx[...] = total.astype(BF16)

    def folded(values):
        rows = jnp.sum((values * values).reshape(-1, 8, values.shape[1]), axis=0)
        out = rows[:, 0:128]
        for i in range(1, values.shape[1] // 128):
            out += rows[:, 128 * i : 128 * (i + 1)]
        return out

    sq[0] = jnp.zeros((8, 128), F32)
    for j in range(2):
        arrived(gr_in.at[j], grs.at[j])
        summed = acc_in[j] + gr_in[j].astype(F32)
        acc_in[j] = summed
        sq[0] += folded(summed)
        arrived(gr_out.at[j], grs.at[2 + j])
        summed = acc_out[j] + gr_out[j].astype(F32)
        acc_out[j] = summed
        sq[0] += folded(summed)

    for slot, where in group_one:
        put(sq.at[0], sqr1.at[slot], s1s.at[slot], s1r.at[slot], where)
    whole = sq[0]
    for slot, _ in group_one:
        arrived(sqr1.at[slot], s1r.at[slot])
        whole += sqr1[slot]
    sq[1] = whole
    for slot, where in group_two:
        put(sq.at[1], sqr2.at[slot], s2s.at[slot], s2r.at[slot], where)
    for slot, _ in group_two:
        arrived(sqr2.at[slot], s2r.at[slot])
        whole += sqr2[slot]
    factor = lax.rsqrt(jnp.sum(whole, keepdims=True) / (2.0 * D * FW) + 1e-06)
    for j in range(2):
        o_gin[:, j * Q : (j + 1) * Q] = (acc_in[j] * factor).astype(BF16)
        o_gout[j * Q : (j + 1) * Q, :] = (acc_out[j] * factor).astype(BF16)

    @pl.loop(0, NB)
    def _(b):
        for k in (0, 1, 2, 3, 4, 5, 9, 10):
            left(got.at[0, 0], ss.at[b, k])
        for k in (6, 7, 8):
            left(full.at[0, 0], ss.at[b, k])

        @pl.when(b > 0)
        def _():
            left(dxs.at[0, 0:HALF], ss.at[b, 11])
            left(xall.at[0], ss.at[b, 13])

        left(dxs.at[0, 0:HALF], ss.at[b, 12])

    left(xall.at[0, :, 0:HALF], ss.at[0, 13])
    for j in range(2):
        left(wsib.at[j], wss.at[j])
        left(gs_in.at[j], gss.at[j])
        left(gs_out.at[j], gss.at[2 + j])
    for slot, _ in group_one:
        left(sq.at[0], s1s.at[slot])
    for slot, _ in group_two:
        left(sq.at[1], s2s.at[slot])


def shards(tokens, w_in, w_out, out_grad):
    vmem = pl.BlockSpec(memory_space=pltpu.VMEM)
    dma = pltpu.SemaphoreType.DMA
    return pl.pallas_call(
        kernel,
        out_shape=(
            jax.ShapeDtypeStruct((HALF, W), BF16),
            jax.ShapeDtypeStruct((W, W), BF16),
            jax.ShapeDtypeStruct((W, W), BF16),
        ),
        in_specs=[vmem] * 4,
        out_specs=(vmem,) * 3,
        scratch_shapes=[
            pltpu.VMEM((NB, 2, ROWS, W), BF16),
            pltpu.VMEM((2, W, W), BF16),
            pltpu.VMEM((NB, 4, 2, ROWS, Q), BF16),
            pltpu.VMEM((NB, 6, ROWS, Q), BF16),
            pltpu.VMEM((NB, 2, ROWS, Q), BF16),
            pltpu.VMEM((NB, 4, 2, ROWS, Q), BF16),
            pltpu.VMEM((4, W, Q), F32),
            pltpu.VMEM((4, Q, W), F32),
            pltpu.VMEM((NB, ROWS, W), BF16),
            pltpu.VMEM((NB, 2, HALF, W), BF16),
            pltpu.VMEM((2, W, Q), BF16),
            pltpu.VMEM((2, Q, W), BF16),
            pltpu.VMEM((2, W, Q), BF16),
            pltpu.VMEM((2, Q, W), BF16),
            pltpu.VMEM((2, 8, 128), F32),
            pltpu.VMEM((16, 8, 128), F32),
            pltpu.VMEM((16, 8, 128), F32),
            dma((NB, 14)), dma((NB, 14)),
            dma((2,)), dma((2,)),
            dma((4,)), dma((4,)),
            dma((16,)), dma((16,)),
            dma((16,)), dma((16,)),
        ],
        compiler_params=pltpu.CompilerParams(
            collective_id=0, has_side_effects=True, vmem_limit_bytes=60 * 2**20
        ),
        cost_estimate=pl.CostEstimate(
            flops=12_100_000_000, bytes_accessed=10_000_000, transcendentals=400_000
        ),
    )(tokens, w_in, w_out, out_grad)


def solution(mesh):
    placed = (
        P(("gy", "gx"), "gz"),
        P("gz", ("gx", "gy")),
        P(("gx", "gy"), "gz"),
        P(("gy", "gx"), "gz"),
    )
    return jax.shard_map(
        shards,
        mesh=mesh,
        in_specs=placed,
        out_specs=(P(("gy", "gx"), "gz"), P("gz", ("gx", "gy")), P(("gx", "gy"), "gz")),
        check_vma=False,
    )
```

time: 640 us -> 174 us (0.27)
  waiting for transfers between devices: 452 us -> 0 us
  Pallas kernels: 0 us -> 168 us
  blocking collectives: 125 us -> 0 us
  matrix products: 31.5 us -> 0 us
  between operations: 15.9 us -> 0.64 us
  other arithmetic: 9.35 us -> 0 us
    reduce_scatter x5 -> x0, waiting for transfers between devices: 261 us -> none  [the longest x1 87.2 us: shards(): lax.psum_scatter(h_term.astype(jnp.bfloat16), 'gz', scatter_dimension=0,...]
    all_gather x4 -> x0, waiting for transfers between devices: 189 us -> none  [the longest x1 67.2 us: shards(): lax.all_gather(d_pre, 'gz', axis=0, tiled=True)]
    pallas_call x0 -> x1, Pallas kernels: none -> 168 us  [shards(): pl.pallas_call(kernel, out_shape=(jax.ShapeDtypeStruct((HALF, W), BF16),...]
    psum x1 -> x0, blocking collectives: 77.4 us -> none  [shards(): grand_total = lax.psum(local_square, ('gx', 'gy', 'gz'))]
    all_gather x2 -> x0, blocking collectives: 48 us -> none  [the longest x1 24.8 us: shards(): lax.all_gather(out_grad, 'gx', axis=0, tiled=True)]
    dot_general x5 -> x0, matrix products: 31.5 us -> none  [contract(): lax.dot_general(left, right, (((left_dim,), (right_dim,)), ((), ())), pre...]
  transfers between devices with their start and end apart: 9 -> 0, of which waited for: 8 -> 0; matrix products, arithmetic and copies ran while one was open for 6% -> 0% of each run, Pallas kernels for 0% -> 0%
where the time goes in v1:
time: 174 us; the launch traced here: 173 us
  Pallas kernels  168 us (97%)
  local copies, waits for them, and re-layouts  5.01 us (3%)
    pallas_call x1, Pallas kernels, shards(): pl.pallas_call(kernel, out_shape=(jax.ShapeDtypeStruct((HALF, W), BF16),...  168 us
    unnamed x5, local copies, waits for them, and re-layouts  5.01 us

profile of v1, /device:TPU:1, one launch (start us, length us, event | category | flops | bytes accessed | tf_op | source)
XLA Modules:
  0.0 173.4 jit_solution(3486450291020124505)
XLA Ops:
  0.6 167.7 %shard_map.67 = (bf16[64,768]{1,0:T(8,128)(2,1)}, bf16[768,768]{1,0:T(8,128)(2,1)}, bf16[768,768]{1,0:T(8,128)(2,1)}) custom-call(bf16[64,768]{1,0:T(8,128)(2,1)} %tok.1, bf16[768,768]{1,0:T(8,128)(2,1)} %win.1, bf16[768,768]{1,0:T(8,128)(2,1)} %wout.1, bf16[64,768]{1,0:T(8,128)(2,1)} %dy.1), custom_call_target="tpu_custom_call" | custom-call | flops 12099999744 | bytes 10000000 | tf_op jit(solution)/shard_map/pallas_call | solution.py:294
  168.4 1.5 copy.10
  169.9 0.0 copy-start
  169.9 2.5 %copy.11 = bf16[768,768]{1,0:T(8,128)(2,1)} copy(bf16[768,768]{1,0:T(8,128)(2,1)} %get-tuple-element.7) | data formatting | bytes 2359296
  172.4 0.0 copy-done
  172.4 1.0 copy.12
Async XLA Ops:
  169.9 2.5 %copy-start = (bf16[768,768]{1,0:T(8,128)(2,1)S(1)}, bf16[768,768]{1,0:T(8,128)(2,1)}, u32[]{:S(2)}) copy-start(bf16[768,768]{1,0:T(8,128)(2,1)} %get-tuple-element.8) | copy-start | bytes 3538948

commit v2 on v0

v2 whole, which is shorter than its diff:
```python
import jax
import jax.numpy as jnp
from jax import lax
from jax.experimental import pallas as pl
from jax.experimental.pallas import tpu as pltpu
from jax.sharding import PartitionSpec as P

D = 6144
FW = 24576
GELU_C = 0.7978845608
MESH = pl.DeviceIdType.MESH

NB = 8
ROWS = 128
HALF = 64
W = 768
SPLIT = 4
Q = 384
F32 = jnp.float32
BF16 = jnp.bfloat16


def gelu_parts(values):
    square = values * values
    inner_arg = GELU_C * (values + 0.044715 * square * values)
    tanh_val = jnp.tanh(inner_arg)
    value_out = 0.5 * values * (1.0 + tanh_val)
    slope = 0.5 * (1.0 + tanh_val) + 0.5 * values * (1.0 - tanh_val * tanh_val) * GELU_C * (
        1.0 + 3.0 * 0.044715 * square
    )
    return (value_out, slope)


def contract(left, right, left_dim, right_dim):
    return lax.dot_general(
        left, right, (((left_dim,), (right_dim,)), ((), ())), preferred_element_type=F32
    )


def kernel(
    tok, win, wout, dy, o_dx, o_gin, o_gout, o_sum,
    xall, xsib, wown, wsib, part, got, xgot, full, fsib, acc_in, acc_out, dxs, dxr,
    sq, sqr1, sqr2,
    ls, ss, xr, rs, wrs, srs, crs,
):
    z, gy, gz = lax.axis_index("gx"), lax.axis_index("gy"), lax.axis_index("gz")
    yy, xh = gz // 2, gz % 2
    xl, core = gy // 2, gy % 2
    up, down, far = (yy + 1) % 4, (yy + 3) % 4, (yy + 2) % 4
    to_up, to_down = {"gz": up * 2 + xh}, {"gz": down * 2 + xh}
    hi_gz = yy * 2 + 1 - xh
    other_gy = (1 - xl) * 2 + core
    sib_gy = xl * 2 + 1 - core
    to_hi, to_lo, to_sib = {"gz": hi_gz}, {"gy": other_gy}, {"gy": sib_gy}
    z_up, z_down = {"gx": (z + 1) % 8}, {"gx": (z + 7) % 8}

    group_one = [
        (dz * 2 + k, {"gx": (z + dz) % 8, "gy": other_gy if k else gy})
        for dz in range(8) for k in range(2) if dz + k
    ]
    group_two = [
        (d * 4 + kx * 2 + kc, {
            "gz": ((yy + d) % 4) * 2 + (1 - xh if kx else xh),
            "gy": sib_gy if kc else gy,
        })
        for d in range(4) for kx in range(2) for kc in range(2) if d + kx + kc
    ]
    s_sum, s_act, s_pass, s_move, s_core, s_one, s_two, s_half = [ss.at[i] for i in range(8)]

    def put(src, dst, send, recv, where):
        pltpu.make_async_remote_copy(
            src_ref=src, dst_ref=dst, send_sem=send, recv_sem=recv,
            device_id=where, device_id_type=MESH,
        ).start()

    def arrived(ref, sem):
        pltpu.make_async_remote_copy(
            src_ref=ref, dst_ref=ref, send_sem=sem, recv_sem=sem,
            device_id=to_up, device_id_type=MESH,
        ).wait_recv()

    def left(ref, sem):
        pltpu.make_async_remote_copy(
            src_ref=ref, dst_ref=ref, send_sem=sem, recv_sem=sem,
            device_id=to_up, device_id_type=MESH,
        ).wait_send()

    loads = [
        pltpu.make_async_copy(tok, xall.at[0, 0, 0], ls.at[0]),
        pltpu.make_async_copy(dy, xall.at[0, 0, 1], ls.at[1]),
        pltpu.make_async_copy(win, wown.at[0], ls.at[2]),
        pltpu.make_async_copy(wout, wown.at[1], ls.at[3]),
    ]
    for load in loads:
        load.start()
    barrier = pltpu.get_barrier_semaphore()
    for _, where in group_one + group_two:
        pl.semaphore_signal(barrier, inc=1, device_id=where, device_id_type=MESH)
    acc_in[...] = jnp.zeros_like(acc_in)
    acc_out[...] = jnp.zeros_like(acc_out)
    loads[0].wait()
    loads[1].wait()
    pl.semaphore_wait(barrier, 30)

    put(xall.at[0, 0], xall.at[0, 1], s_move, xr.at[0, 1], to_lo)
    put(xall.at[0, 0], xall.at[1, 0], s_move, xr.at[1, 0], z_up)
    put(xall.at[0, 0], xall.at[1, 1], s_move, xr.at[1, 1], z_down)
    loads[2].wait()
    loads[3].wait()
    put(wown.at[0], wsib.at[0], s_core, wrs.at[0], to_sib)
    put(wown.at[1], wsib.at[1], s_core, wrs.at[1], to_sib)

    def one(b, rows, x, g, which, w_in, w_out):
        h = contract(x, w_in, 1, 0).astype(BF16)
        part[b, 2 * which, 0, rows] = h[:, :Q]
        part[b, 2 * which + 1, 0, rows] = h[:, Q:]
        d = contract(g, w_out, 1, 1).astype(BF16)
        part[b, 2 * which, 1, rows] = d[:, :Q]
        part[b, 2 * which + 1, 1, rows] = d[:, Q:]

    def send_products(b, rows):
        put(part.at[b, far, 0, rows], got.at[6 * b, rows], s_sum, rs.at[b, 0], to_up)
        put(part.at[b, far, 1, rows], got.at[6 * b + 1, rows], s_sum, rs.at[b, 0], to_down)
        put(part.at[b, up, 1, rows], got.at[6 * b + 2, rows], s_sum, rs.at[b, 1], to_up)
        put(part.at[b, down, 0, rows], got.at[6 * b + 3, rows], s_sum, rs.at[b, 1], to_down)

    put(xall.at[0, 0], xsib.at[0, 0], s_half, rs.at[0, 6], to_sib)
    low, high, every = slice(0, HALF), slice(HALF, ROWS), slice(0, ROWS)
    one(0, low, xall[0, 0, 0], xall[0, 0, 1], 0, wown[0], wown[1])
    arrived(wsib.at[0], wrs.at[0])
    arrived(wsib.at[1], wrs.at[1])
    one(0, low, xall[0, 0, 0], xall[0, 0, 1], 1, wsib[0], wsib[1])
    send_products(0, low)
    arrived(xall.at[0, 1], xr.at[0, 1])
    put(xall.at[0, 1], xsib.at[0, 1], s_half, rs.at[0, 6], to_sib)
    put(xall.at[0, 1], xall.at[7, 0], s_move, xr.at[7, 0], z_up)
    put(xall.at[0, 1], xall.at[7, 1], s_move, xr.at[7, 1], z_down)
    for k, w in enumerate((wown, wsib)):
        one(0, high, xall[0, 1, 0], xall[0, 1, 1], k, w[0], w[1])
    send_products(0, high)

    def products(b):
        @pl.when(b < 5)
        def _():
            arrived(xall.at[b, 0], xr.at[b, 0])

            @pl.when(b < 4)
            def _():
                put(xall.at[b, 0], xall.at[b + 1, 0], s_move, xr.at[b + 1, 0], z_up)

            arrived(xall.at[b, 1], xr.at[b, 1])

            @pl.when(b < 3)
            def _():
                put(xall.at[b, 1], xall.at[b + 1, 1], s_move, xr.at[b + 1, 1], z_down)

        x = xall[b, :, 0].reshape(ROWS, W)
        g = xall[b, :, 1].reshape(ROWS, W)
        for k, w in enumerate((wown, wsib)):
            one(b, every, x, g, k, w[0], w[1])
        send_products(b, every)
        put(xall.at[b], xsib.at[b], s_half, rs.at[b, 6], to_sib)

    def forward(t):
        s = 8 - t
        arrived(xall.at[s, 1], xr.at[s, 1])
        put(xall.at[s, 1], xall.at[s - 1, 1], s_move, xr.at[s - 1, 1], z_down)
        arrived(xall.at[s, 0], xr.at[s, 0])

        @pl.when(t < 3)
        def _():
            put(xall.at[s, 0], xall.at[s - 1, 0], s_move, xr.at[s - 1, 0], z_up)

    def relay_sums(b):
        arrived(got.at[pl.ds(6 * b, 2)], rs.at[b, 0])
        part[b, up, 0] = (part[b, up, 0].astype(F32) + got[6 * b].astype(F32)).astype(BF16)
        put(part.at[b, up, 0], got.at[6 * b + 4], s_sum, rs.at[b, 1], to_up)
        part[b, down, 1] = (
            part[b, down, 1].astype(F32) + got[6 * b + 1].astype(F32)
        ).astype(BF16)
        put(part.at[b, down, 1], got.at[6 * b + 5], s_sum, rs.at[b, 1], to_down)

    def quarter_sums(b):
        arrived(got.at[pl.ds(6 * b + 2, 4)], rs.at[b, 1])
        part[b, yy, 0] = (
            part[b, yy, 0].astype(F32) + got[6 * b + 3].astype(F32) + got[6 * b + 4].astype(F32)
        ).astype(BF16)
        part[b, yy, 1] = (
            part[b, yy, 1].astype(F32) + got[6 * b + 2].astype(F32) + got[6 * b + 5].astype(F32)
        ).astype(BF16)
        put(part.at[b, yy], xgot.at[b], s_act, rs.at[b, 2], to_hi)

    def activate(b):
        arrived(xgot.at[b], rs.at[b, 2])
        value_out, slope = gelu_parts(part[b, yy, 0].astype(F32) + xgot[b, 0].astype(F32))
        d_pre = (part[b, yy, 1].astype(F32) + xgot[b, 1].astype(F32)) * slope
        full[b, yy, :, 0] = value_out.astype(BF16).reshape(2, HALF, Q)
        full[b, yy, :, 1] = d_pre.astype(BF16).reshape(2, HALF, Q)

        @pl.when(b < SPLIT)
        def _():
            mine = full.at[b, yy, xh]
            put(mine, mine, s_act, rs.at[b, 3], to_up)
            put(mine, mine, s_act, rs.at[b, 3], to_down)

        @pl.when(b >= SPLIT)
        def _():
            mine = full.at[b, yy]
            put(mine, mine, s_act, rs.at[b, 3], to_up)
            put(mine, mine, s_act, rs.at[b, 3], to_down)

    def relay_acts(b):
        @pl.when(b < SPLIT)
        def _():
            arrived(full.at[b, 0], rs.at[b, 3])
            low, high = full.at[b, down, xh], full.at[b, up, xh]
            put(low.at[0], low.at[0], s_pass, rs.at[b, 4], to_up)
            put(high.at[1], high.at[1], s_pass, rs.at[b, 4], to_down)
            put(low, low, s_pass, rs.at[b, 5], to_hi)
            put(high, high, s_pass, rs.at[b, 5], to_hi)

        @pl.when(b >= SPLIT)
        def _():
            arrived(full.at[b, 0:2], rs.at[b, 3])
            low, high = full.at[b, down, :, 0], full.at[b, up, :, 1]
            put(low, low, s_pass, rs.at[b, 4], to_up)
            put(high, high, s_pass, rs.at[b, 4], to_down)

    def far_acts(b):
        mine = full.at[b, far, xh]
        arrived(mine, rs.at[b, 4])
        put(mine, mine, s_pass, rs.at[b, 5], to_hi)

    def input_grad(b, ready, sem):
        arrived(ready, sem)
        put(full.at[b, 2:4], fsib.at[b], s_half, rs.at[b, 6], to_sib)
        own, sib = [
            jnp.concatenate([full[b, q, :, 1].reshape(ROWS, Q) for q in qs], axis=1)
            for qs in ((0, 1), (2, 3))
        ]
        partial = contract(own, wown[0], 1, 1) + contract(sib, wsib[0], 1, 1)

        @pl.when(b < 4)
        def _():
            dxs[b] = partial.astype(BF16)

            @pl.when(b > 0)
            def _():
                put(dxs.at[b, low], dxr.at[2 * b], s_pass, srs.at[2], {"gx": (z + 8 - b) % 8})
                put(dxs.at[b, high], dxr.at[2 * b + 1], s_pass, srs.at[2], {"gx": (z + b) % 8})

            @pl.when(b == 0)
            def _():
                put(dxs.at[0, high], dxr.at[1], s_pass, srs.at[2], to_lo)

        @pl.when(b == 4)
        def _():
            dxs[b] = partial.astype(BF16)
            put(dxs.at[4, low], dxr.at[8], s_pass, srs.at[2], {"gx": (z + 4) % 8})
            put(dxs.at[4, high], dxr.at[11], s_pass, crs.at[0, 1], z_up)

        @pl.when(b > 4)
        def _():
            arrived(dxr.at[2 * b + 1], crs.at[b - 5, 1])
            dxs[b, high] = (partial[HALF:] + dxr[2 * b + 1].astype(F32)).astype(BF16)

            @pl.when(b == 5)
            def _():
                dxs[b, low] = partial[:HALF].astype(BF16)

            @pl.when(b > 5)
            def _():
                arrived(dxr.at[2 * b], crs.at[b - 5, 0])
                dxs[b, low] = (partial[:HALF] + dxr[2 * b].astype(F32)).astype(BF16)

            @pl.when(b < NB - 1)
            def _():
                put(dxs.at[b, low], dxr.at[2 * b + 2], s_pass, crs.at[b - 4, 0], z_down)
                put(dxs.at[b, high], dxr.at[2 * b + 3], s_pass, crs.at[b - 4, 1], z_up)

            @pl.when(b == NB - 1)
            def _():
                put(
                    dxs.at[b, low], dxr.at[9], s_pass, srs.at[2],
                    {"gx": (z + 7) % 8, "gy": other_gy},
                )
                put(
                    dxs.at[b, high], dxr.at[10], s_pass, srs.at[2],
                    {"gx": (z + 1) % 8, "gy": other_gy},
                )

    def input_grad_split(b):
        input_grad(b, full.at[b, 0:3, 0], rs.at[b, 5])

    def input_grad_whole(b):
        input_grad(b, full.at[b, far], rs.at[b, 4])

    def pair(tokens, acts, first):
        x = tokens[pl.ds(first, 2), :, 0].reshape(2 * ROWS, W)
        g = tokens[pl.ds(first, 2), :, 1].reshape(2 * ROWS, W)
        act = [acts[pl.ds(first, 2), q, :, 0].reshape(2 * ROWS, Q) for q in range(2)]
        d_pre = [acts[pl.ds(first, 2), q, :, 1].reshape(2 * ROWS, Q) for q in range(2)]
        return x, g, act, d_pre

    def weight_grads(parts):
        x_t = jnp.concatenate([part[0] for part in parts], axis=0).T
        g = jnp.concatenate([part[1] for part in parts], axis=0)
        for q in range(2):
            act_t = jnp.concatenate([part[2][q] for part in parts], axis=0).T
            d_pre = jnp.concatenate([part[3][q] for part in parts], axis=0)
            acc_in[q] += contract(x_t, d_pre, 1, 0)
            acc_out[q] += contract(act_t, g, 1, 0)

    def sibling_done(b):
        arrived(got.at[0:8], rs.at[b, 6])

    stages = (
        (5, NB, 0, products), (0, NB, 1, relay_sums), (0, NB, 2, quarter_sums),
        (0, NB, 3, activate), (0, NB, 4, relay_acts), (0, SPLIT, 5, far_acts),
        (0, SPLIT, 6, input_grad_split), (SPLIT, NB, 5, input_grad_whole),
        (1, 5, 0, products),
    )

    @pl.loop(1, NB + 5)
    def _(t):
        for first, end, lag, stage in stages:
            b = t - lag

            @pl.when((b >= first) & (b < end))
            def _(stage=stage, b=b):
                stage(b)

        @pl.when(t < 4)
        def _():
            forward(t)

        last = t - 6

        @pl.when((last >= 0) & (last < NB - 1) & (last % 2 == 1))
        def _():
            sibling_done(last - 1)
            sibling_done(last)
            weight_grads([pair(xall, full, last - 1), pair(xsib, fsib, last - 1)])

    weight_grads([pair(xall, full, NB - 2)])
    sibling_done(NB - 2)
    sibling_done(NB - 1)
    weight_grads([pair(xsib, fsib, NB - 2)])

    def folded(values):
        rows = jnp.sum((values * values).reshape(-1, 8, values.shape[1]), axis=0)
        out = rows[:, 0:128]
        for i in range(1, values.shape[1] // 128):
            out += rows[:, 128 * i : 128 * (i + 1)]
        return out

    squares = jnp.zeros((8, 128), F32)
    stores = []
    for j in range(2):
        squares += folded(acc_in[j]) + folded(acc_out[j])
        stores.append(pltpu.make_async_copy(acc_in.at[j], o_gin.at[:, j * Q : (j + 1) * Q], ls.at[j]))
        stores.append(pltpu.make_async_copy(acc_out.at[j], o_gout.at[j * Q : (j + 1) * Q], ls.at[2 + j]))
    sq[0] = squares

    for slot, where in group_two:
        put(sq.at[0], sqr1.at[slot], s_one, srs.at[0], where)
    for store in stores:
        store.start()
    arrived(sqr1.at[1:16], srs.at[0])
    whole = sq[0] + jnp.sum(sqr1[1:16], axis=0)
    sq[1] = whole
    for slot, where in group_one:
        put(sq.at[1], sqr2.at[slot], s_two, srs.at[1], where)

    arrived(dxr.at[1:11], srs.at[2])
    total = dxs[0, 0:HALF].astype(F32)
    for i in range(1, 11):
        total += dxr[i].astype(F32)
    o_dx[...] = total.astype(BF16)

    arrived(sqr2.at[1:16], srs.at[1])
    o_sum[...] = whole + jnp.sum(sqr2[1:16], axis=0)

    for store in stores:
        store.wait()
    left(got.at[0:48], s_sum)
    left(got.at[0 : 16 + 2 * (16 - SPLIT)], s_act)
    left(got.at[0 : (16 - SPLIT) + 3 * SPLIT + 15], s_pass)
    left(got.at[0:30], s_move)
    left(got.at[0:24], s_core)
    left(part, s_half)
    left(sqr1.at[1:16], s_one)
    left(sqr2.at[1:16], s_two)


def scale_kernel(squares, dx, gin, gout, o_dx, o_gin, o_gout):
    total = jnp.sum(squares[...], keepdims=True)
    factor = 1.0 / jnp.sqrt(total / (2.0 * D * FW) + 1e-06)
    o_dx[...] = dx[...]
    o_gin[...] = (gin[...] * factor).astype(BF16)
    o_gout[...] = (gout[...] * factor).astype(BF16)


def scaled(squares, in_grad, grad_in, grad_out):
    steps = 4
    fixed = lambda shape: pl.BlockSpec(shape, lambda i: (0, 0))
    moving = lambda: pl.BlockSpec((W // steps, W), lambda i: (i, 0))
    return pl.pallas_call(
        scale_kernel,
        grid=(steps,),
        out_shape=(
            jax.ShapeDtypeStruct((HALF, W), BF16),
            jax.ShapeDtypeStruct((W, W), BF16),
            jax.ShapeDtypeStruct((W, W), BF16),
        ),
        in_specs=[fixed((8, 128)), fixed((HALF, W)), moving(), moving()],
        out_specs=(fixed((HALF, W)), moving(), moving()),
    )(squares, in_grad, grad_in, grad_out)


def shards(tokens, w_in, w_out, out_grad):
    vmem = pl.BlockSpec(memory_space=pltpu.VMEM)
    hbm = pl.BlockSpec(memory_space=pl.ANY)
    dma = pltpu.SemaphoreType.DMA
    in_grad, grad_in, grad_out, squares = pl.pallas_call(
        kernel,
        out_shape=(
            jax.ShapeDtypeStruct((HALF, W), BF16),
            jax.ShapeDtypeStruct((W, W), F32),
            jax.ShapeDtypeStruct((W, W), F32),
            jax.ShapeDtypeStruct((8, 128), F32),
        ),
        in_specs=[hbm] * 4,
        out_specs=(vmem, hbm, hbm, vmem),
        scratch_shapes=[
            pltpu.VMEM((NB, 2, 2, HALF, W), BF16),
            pltpu.VMEM((NB, 2, 2, HALF, W), BF16),
            pltpu.VMEM((2, W, W), BF16),
            pltpu.VMEM((2, W, W), BF16),
            pltpu.VMEM((NB, 4, 2, ROWS, Q), BF16),
            pltpu.VMEM((NB * 6, ROWS, Q), BF16),
            pltpu.VMEM((NB, 2, ROWS, Q), BF16),
            pltpu.VMEM((NB, 4, 2, 2, HALF, Q), BF16),
            pltpu.VMEM((NB, 2, 2, 2, HALF, Q), BF16),
            pltpu.VMEM((2, W, Q), F32),
            pltpu.VMEM((2, Q, W), F32),
            pltpu.VMEM((NB, ROWS, W), BF16),
            pltpu.VMEM((16, HALF, W), BF16),
            pltpu.VMEM((2, 8, 128), F32),
            pltpu.VMEM((16, 8, 128), F32),
            pltpu.VMEM((16, 8, 128), F32),
            dma((4,)),
            dma((8,)),
            dma((NB, 2)),
            dma((NB, 7)),
            dma((2,)),
            dma((3,)),
            dma((3, 2)),
        ],
        compiler_params=pltpu.CompilerParams(
            collective_id=0, has_side_effects=True, vmem_limit_bytes=60 * 2**20
        ),
        cost_estimate=pl.CostEstimate(
            flops=12_100_000_000, bytes_accessed=10_000_000, transcendentals=400_000
        ),
    )(tokens, w_in, w_out, out_grad)
    return scaled(squares, in_grad, grad_in, grad_out)


def solution(mesh):
    placed = (
        P(("gy", "gx"), "gz"),
        P("gz", ("gx", "gy")),
        P(("gx", "gy"), "gz"),
        P(("gy", "gx"), "gz"),
    )
    return jax.shard_map(
        shards,
        mesh=mesh,
        in_specs=placed,
        out_specs=(P(("gy", "gx"), "gz"), P("gz", ("gx", "gy")), P(("gx", "gy"), "gz")),
        check_vma=False,
    )
```

time: 640 us -> 136 us (0.21)
  waiting for transfers between devices: 452 us -> 0 us
  Pallas kernels: 0 us -> 135 us
  blocking collectives: 125 us -> 0 us
  matrix products: 31.5 us -> 0 us
  between operations: 15.9 us -> 0.64 us
  other arithmetic: 9.35 us -> 0 us
    reduce_scatter x5 -> x0, waiting for transfers between devices: 261 us -> none  [the longest x1 87.2 us: shards(): lax.psum_scatter(h_term.astype(jnp.bfloat16), 'gz', scatter_dimension=0,...]
    all_gather x4 -> x0, waiting for transfers between devices: 189 us -> none  [the longest x1 67.2 us: shards(): lax.all_gather(d_pre, 'gz', axis=0, tiled=True)]
    pallas_call x0 -> x2, Pallas kernels: none -> 135 us  [the longest x1 131 us: shards(): pl.pallas_call(kernel, out_shape=(jax.ShapeDtypeStruct((HALF, W), BF16),...]
    psum x1 -> x0, blocking collectives: 77.4 us -> none  [shards(): grand_total = lax.psum(local_square, ('gx', 'gy', 'gz'))]
    all_gather x2 -> x0, blocking collectives: 48 us -> none  [the longest x1 24.8 us: shards(): lax.all_gather(out_grad, 'gx', axis=0, tiled=True)]
    dot_general x5 -> x0, matrix products: 31.5 us -> none  [contract(): lax.dot_general(left, right, (((left_dim,), (right_dim,)), ((), ())), pre...]
  transfers between devices with their start and end apart: 9 -> 0, of which waited for: 8 -> 0; matrix products, arithmetic and copies ran while one was open for 6% -> 0% of each run, Pallas kernels for 0% -> 0%
where the time goes in v2:
time: 136 us
  Pallas kernels  135 us (99%)
    pallas_call x1, Pallas kernels, shards(): pl.pallas_call(kernel, out_shape=(jax.ShapeDtypeStruct((HALF, W), BF16),...  131 us
    pallas_call x1, Pallas kernels, scaled(): pl.pallas_call(scale_kernel, grid=(steps,), out_shape=(jax.ShapeDtypeStru...  4.59 us

profile of v2, /device:TPU:1, one launch (start us, length us, event | category | flops | bytes accessed | tf_op | source)
XLA Modules:
  0.0 135.8 jit_solution(4509105054247320283)
XLA Ops:
  0.6 130.6 %shard_map.67 = (bf16[64,768]{1,0:T(8,128)(2,1)}, f32[768,768]{1,0:T(8,128)}, f32[768,768]{1,0:T(8,128)}, f32[8,128]{1,0:T(8,128)}) custom-call(bf16[64,768]{1,0:T(8,128)(2,1)} %tok.1, bf16[768,768]{1,0:T(8,128)(2,1)} %win.1, bf16[768,768]{1,0:T(8,128)(2,1)} %wout.1, bf16[64,768]{1,0:T(8,128)(2,1)} %dy.1), custom_call_target="tpu_custom_call" | custom-call | flops 12099999744 | bytes 10000000 | tf_op jit(solution)/shard_map/pallas_call | solution.py:425
  131.3 4.6 %shard_map.68 = (bf16[64,768]{1,0:T(8,128)(2,1)}, bf16[768,768]{1,0:T(8,128)(2,1)}, bf16[768,768]{1,0:T(8,128)(2,1)}) custom-call(f32[8,128]{1,0:T(8,128)} %get-tuple-element.7.squares, bf16[64,768]{1,0:T(8,128)(2,1)} %get-tuple-element.8.dx, f32[768,768]{1,0:T(8,128)} %get-tuple-element.9.gin, f32[768,768]{1,0:T(8,128)} %get-tuple-element.10.gout), custom_call_target="tpu_custom_call" | custom-call | tf_op jit(solution)/shard_map/pallas_call | solution.py:408

commit v3 on v2

v3 whole, which is shorter than its diff:
```python
import jax
import jax.numpy as jnp
from jax import lax
from jax.experimental import pallas as pl
from jax.experimental.pallas import tpu as pltpu
from jax.sharding import PartitionSpec as P

D = 6144
FW = 24576
GELU_C = 0.7978845608
MESH = pl.DeviceIdType.MESH

NB = 16
ROWS = 64
HALF = 32
W = 768
SPLIT, EVERY, OF = 14, 2, 1
Q = 384
F32 = jnp.float32
BF16 = jnp.bfloat16


def gelu_parts(values):
    square = values * values
    inner_arg = GELU_C * (values + 0.044715 * square * values)
    tanh_val = jnp.tanh(inner_arg)
    value_out = 0.5 * values * (1.0 + tanh_val)
    slope = 0.5 * (1.0 + tanh_val) + 0.5 * values * (1.0 - tanh_val * tanh_val) * GELU_C * (
        1.0 + 3.0 * 0.044715 * square
    )
    return (value_out, slope)


def contract(left, right, left_dim, right_dim):
    return lax.dot_general(
        left, right, (((left_dim,), (right_dim,)), ((), ())), preferred_element_type=F32
    )


def kernel(
    tok, win, wout, dy, o_dx, o_gin, o_gout, o_sum,
    xall, xsib, wown, wsib, part, got, xgot, full, fsib, acc_in, acc_out, out_in, out_out, dxs, dxr,
    sq, sqr1, sqr2,
    ls, ss, xr, rs, wrs, srs, crs,
):
    z, gy, gz = lax.axis_index("gx"), lax.axis_index("gy"), lax.axis_index("gz")
    yy, xh = gz // 2, gz % 2
    xl, core = gy // 2, gy % 2
    up, down, far = (yy + 1) % 4, (yy + 3) % 4, (yy + 2) % 4
    to_up, to_down = {"gz": up * 2 + xh}, {"gz": down * 2 + xh}
    hi_gz = yy * 2 + 1 - xh
    other_gy = (1 - xl) * 2 + core
    sib_gy = xl * 2 + 1 - core
    to_hi, to_lo, to_sib = {"gz": hi_gz}, {"gy": other_gy}, {"gy": sib_gy}
    z_up, z_down = {"gx": (z + 1) % 8}, {"gx": (z + 7) % 8}

    group_one = [
        (dz * 2 + k, {"gx": (z + dz) % 8, "gy": other_gy if k else gy})
        for dz in range(8) for k in range(2) if dz + k
    ]
    group_two = [
        (d * 4 + kx * 2 + kc, {
            "gz": ((yy + d) % 4) * 2 + (1 - xh if kx else xh),
            "gy": sib_gy if kc else gy,
        })
        for d in range(4) for kx in range(2) for kc in range(2) if d + kx + kc
    ]
    s_sum, s_act, s_pass, s_move, s_core, s_one, s_two, s_half = [ss.at[i] for i in range(8)]

    def put(src, dst, send, recv, where):
        pltpu.make_async_remote_copy(
            src_ref=src, dst_ref=dst, send_sem=send, recv_sem=recv,
            device_id=where, device_id_type=MESH,
        ).start()

    def arrived(ref, sem):
        pltpu.make_async_remote_copy(
            src_ref=ref, dst_ref=ref, send_sem=sem, recv_sem=sem,
            device_id=to_up, device_id_type=MESH,
        ).wait_recv()

    def left(ref, sem):
        pltpu.make_async_remote_copy(
            src_ref=ref, dst_ref=ref, send_sem=sem, recv_sem=sem,
            device_id=to_up, device_id_type=MESH,
        ).wait_send()

    loads = [
        pltpu.make_async_copy(tok, xall.at[0, 0, 0], ls.at[0]),
        pltpu.make_async_copy(dy, xall.at[0, 0, 1], ls.at[1]),
        pltpu.make_async_copy(win, wown.at[0], ls.at[2]),
        pltpu.make_async_copy(wout, wown.at[1], ls.at[3]),
    ]
    for load in loads:
        load.start()
    barrier = pltpu.get_barrier_semaphore()
    for _, where in group_one + group_two:
        pl.semaphore_signal(barrier, inc=1, device_id=where, device_id_type=MESH)
    acc_in[...] = jnp.zeros_like(acc_in)
    acc_out[...] = jnp.zeros_like(acc_out)
    loads[0].wait()
    loads[1].wait()
    pl.semaphore_wait(barrier, 30)

    put(xall.at[0, 0], xall.at[0, 1], s_move, xr.at[0, 1], to_lo)
    put(xall.at[0, 0], xall.at[1, 0], s_move, xr.at[1, 0], z_up)
    put(xall.at[0, 0], xall.at[1, 1], s_move, xr.at[1, 1], z_down)
    loads[2].wait()
    loads[3].wait()
    put(wown.at[0], wsib.at[0], s_core, wrs.at[0], to_sib)
    put(wown.at[1], wsib.at[1], s_core, wrs.at[1], to_sib)

    def one(b, x, g, which, w_in, w_out):
        h = contract(x, w_in, 1, 0).astype(BF16)
        part[b, 2 * which, 0] = h[:, :Q]
        part[b, 2 * which + 1, 0] = h[:, Q:]
        d = contract(g, w_out, 1, 1).astype(BF16)
        part[b, 2 * which, 1] = d[:, :Q]
        part[b, 2 * which + 1, 1] = d[:, Q:]

    def send_products(b):
        put(part.at[b, far, 0], got.at[6 * b], s_sum, rs.at[b, 0], to_up)
        put(part.at[b, far, 1], got.at[6 * b + 1], s_sum, rs.at[b, 0], to_down)
        put(part.at[b, up, 1], got.at[6 * b + 2], s_sum, rs.at[b, 1], to_up)
        put(part.at[b, down, 0], got.at[6 * b + 3], s_sum, rs.at[b, 1], to_down)

    put(xall.at[0, 0], xsib.at[0, 0], s_half, rs.at[0, 6], to_sib)
    one(0, xall[0, 0, 0], xall[0, 0, 1], 0, wown[0], wown[1])
    arrived(wsib.at[0], wrs.at[0])
    arrived(wsib.at[1], wrs.at[1])
    one(0, xall[0, 0, 0], xall[0, 0, 1], 1, wsib[0], wsib[1])
    send_products(0)

    def products(b):
        slot, side = b // 2, b % 2

        @pl.when(b < 10)
        def _():
            arrived(xall.at[slot, side], xr.at[slot, side])

        @pl.when((b > 1) & (b < 8) & (side == 0))
        def _():
            put(xall.at[slot, 0], xall.at[slot + 1, 0], s_move, xr.at[slot + 1, 0], z_up)

        @pl.when((b > 1) & (b < 6) & (side == 1))
        def _():
            put(xall.at[slot, 1], xall.at[slot + 1, 1], s_move, xr.at[slot + 1, 1], z_down)

        @pl.when(b == 8)
        def _():
            put(xall.at[4, 0], xall.at[4, 1], s_move, xr.at[4, 1], to_lo)

        for k, w in enumerate((wown, wsib)):
            one(b, xall[slot, side, 0], xall[slot, side, 1], k, w[0], w[1])
        send_products(b)
        put(xall.at[slot, side], xsib.at[slot, side], s_half, rs.at[b, 6], to_sib)

    def forward(s):
        arrived(xall.at[s, 0], xr.at[s, 0])
        put(xall.at[s, 0], xall.at[s - 1, 0], s_move, xr.at[s - 1, 0], z_up)
        arrived(xall.at[s, 1], xr.at[s, 1])
        put(xall.at[s, 1], xall.at[s - 1, 1], s_move, xr.at[s - 1, 1], z_down)

    def relay_sums(b):
        arrived(got.at[pl.ds(6 * b, 2)], rs.at[b, 0])
        part[b, up, 0] = (part[b, up, 0].astype(F32) + got[6 * b].astype(F32)).astype(BF16)
        put(part.at[b, up, 0], got.at[6 * b + 4], s_sum, rs.at[b, 1], to_up)
        part[b, down, 1] = (
            part[b, down, 1].astype(F32) + got[6 * b + 1].astype(F32)
        ).astype(BF16)
        put(part.at[b, down, 1], got.at[6 * b + 5], s_sum, rs.at[b, 1], to_down)

    def quarter_sums(b):
        arrived(got.at[pl.ds(6 * b + 2, 4)], rs.at[b, 1])
        part[b, yy, 0] = (
            part[b, yy, 0].astype(F32) + got[6 * b + 3].astype(F32) + got[6 * b + 4].astype(F32)
        ).astype(BF16)
        part[b, yy, 1] = (
            part[b, yy, 1].astype(F32) + got[6 * b + 2].astype(F32) + got[6 * b + 5].astype(F32)
        ).astype(BF16)
        put(part.at[b, yy], xgot.at[b], s_act, rs.at[b, 2], to_hi)

    def in_split(b):
        return (b < SPLIT) & (b % EVERY < OF)

    def activate(b):
        arrived(xgot.at[b], rs.at[b, 2])
        value_out, slope = gelu_parts(part[b, yy, 0].astype(F32) + xgot[b, 0].astype(F32))
        d_pre = (part[b, yy, 1].astype(F32) + xgot[b, 1].astype(F32)) * slope
        full[b, yy, :, 0] = value_out.astype(BF16).reshape(2, HALF, Q)
        full[b, yy, :, 1] = d_pre.astype(BF16).reshape(2, HALF, Q)

        @pl.when(in_split(b))
        def _():
            mine = full.at[b, yy, xh]
            put(mine, mine, s_act, rs.at[b, 3], to_up)
            put(mine, mine, s_act, rs.at[b, 3], to_down)

        @pl.when(jnp.logical_not(in_split(b)))
        def _():
            mine = full.at[b, yy]
            put(mine, mine, s_act, rs.at[b, 3], to_up)
            put(mine, mine, s_act, rs.at[b, 3], to_down)

    def relay_acts(b):
        @pl.when(in_split(b))
        def _():
            arrived(full.at[b, 0], rs.at[b, 3])
            low, high = full.at[b, down, xh], full.at[b, up, xh]
            put(low.at[0], low.at[0], s_pass, rs.at[b, 4], to_up)
            put(high.at[1], high.at[1], s_pass, rs.at[b, 4], to_down)
            put(low, low, s_pass, rs.at[b, 5], to_hi)
            put(high, high, s_pass, rs.at[b, 5], to_hi)

        @pl.when(jnp.logical_not(in_split(b)))
        def _():
            arrived(full.at[b, 0:2], rs.at[b, 3])
            low, high = full.at[b, down, :, 0], full.at[b, up, :, 1]
            put(low, low, s_pass, rs.at[b, 4], to_up)
            put(high, high, s_pass, rs.at[b, 4], to_down)

    def far_acts(b):
        mine = full.at[b, far, xh]
        arrived(mine, rs.at[b, 4])
        put(mine, mine, s_pass, rs.at[b, 5], to_hi)

    def acts_ready(b, ready, sem):
        arrived(ready, sem)
        put(full.at[b, 2:4], fsib.at[b], s_half, rs.at[b, 6], to_sib)

    def input_grad(b):
        own, sib = [
            jnp.concatenate([full[b, q, :, 1].reshape(ROWS, Q) for q in qs], axis=1)
            for qs in ((0, 1), (2, 3))
        ]
        partial = contract(own, wown[0], 1, 1) + contract(sib, wsib[0], 1, 1)

        slot, side = b // 2, b % 2

        @pl.when(b < 8)
        def _():
            dxs[b] = partial.astype(BF16)

            @pl.when((b > 1) & (side == 0))
            def _():
                put(dxs.at[b], dxr.at[b], s_pass, srs.at[2], {"gx": (z + 8 - slot) % 8})

            @pl.when((b > 1) & (side == 1))
            def _():
                put(dxs.at[b], dxr.at[b], s_pass, srs.at[2], {"gx": (z + slot) % 8})

            @pl.when(b == 1)
            def _():
                put(dxs.at[1], dxr.at[1], s_pass, srs.at[2], to_lo)

        @pl.when(b == 8)
        def _():
            dxs[b] = partial.astype(BF16)
            put(dxs.at[8], dxr.at[8], s_pass, srs.at[2], {"gx": (z + 4) % 8})

        @pl.when((b == 9) | (b == 10))
        def _():
            dxs[b] = partial.astype(BF16)

        @pl.when(b > 10)
        def _():
            arrived(dxr.at[b], crs.at[b - 11])
            dxs[b] = (partial + dxr[b].astype(F32)).astype(BF16)

        @pl.when((b > 8) & (b < NB - 2) & (side == 0))
        def _():
            put(dxs.at[b], dxr.at[b + 2], s_pass, crs.at[b - 9], z_down)

        @pl.when((b > 8) & (b < NB - 2) & (side == 1))
        def _():
            put(dxs.at[b], dxr.at[b + 2], s_pass, crs.at[b - 9], z_up)

        @pl.when(b == NB - 2)
        def _():
            put(dxs.at[b], dxr.at[9], s_pass, srs.at[2], {"gx": (z + 7) % 8, "gy": other_gy})

        @pl.when(b == NB - 1)
        def _():
            put(dxs.at[b], dxr.at[10], s_pass, srs.at[2], {"gx": (z + 1) % 8, "gy": other_gy})

    def input_grad_split(b):
        acts_ready(b, full.at[b, 0:3, 0], rs.at[b, 5])
        input_grad(b)

    def input_grad_whole(b):
        acts_ready(b, full.at[b, far], rs.at[b, 4])
        input_grad(b)

    def blocks(tokens, acts, first, count):
        if count > 1:
            slots = pl.ds(first // 2, count // 2)
            x = tokens[slots, :, 0].reshape(count * ROWS, W)
            g = tokens[slots, :, 1].reshape(count * ROWS, W)
        else:
            x, g = tokens[first // 2, first % 2, 0], tokens[first // 2, first % 2, 1]
        act = [acts[pl.ds(first, count), q, :, 0].reshape(count * ROWS, Q) for q in range(2)]
        d_pre = [acts[pl.ds(first, count), q, :, 1].reshape(count * ROWS, Q) for q in range(2)]
        return x, g, act, d_pre

    def weight_grads(parts):
        x_t = jnp.concatenate([part[0] for part in parts], axis=0).T
        g = jnp.concatenate([part[1] for part in parts], axis=0)
        for q in range(2):
            act_t = jnp.concatenate([part[2][q] for part in parts], axis=0).T
            d_pre = jnp.concatenate([part[3][q] for part in parts], axis=0)
            acc_in[q] += contract(x_t, d_pre, 1, 0)
            acc_out[q] += contract(act_t, g, 1, 0)

    def sibling_done(b):
        arrived(got.at[0:8], rs.at[b, 6])

    stages = (
        (1, NB, None, 0, products), (0, NB, None, 1, relay_sums), (0, NB, None, 2, quarter_sums),
        (0, NB, None, 3, activate), (0, NB, None, 4, relay_acts), (0, NB, True, 5, far_acts),
        (0, NB, True, 6, input_grad_split), (0, NB - 1, False, 5, input_grad_whole),
    )

    @pl.loop(1, NB + 4)
    def _(t):
        for first, end, split, lag, stage in stages:
            b = t - lag
            runs = (b >= first) & (b < end)
            if split is not None:
                runs = runs & (in_split(b) if split else jnp.logical_not(in_split(b)))

            @pl.when(runs)
            def _(stage=stage, b=b):
                stage(b)

        @pl.when(t == 3)
        def _():
            put(xall.at[0, 1], xall.at[7, 0], s_move, xr.at[7, 0], z_up)
            put(xall.at[0, 1], xall.at[7, 1], s_move, xr.at[7, 1], z_down)

        @pl.when((t == 5) | (t == 7))
        def _():
            forward(7 - (t - 5) // 2)

        @pl.when(t == 9)
        def _():
            arrived(xall.at[5, 0], xr.at[5, 0])
            arrived(xall.at[5, 1], xr.at[5, 1])

        last = t - 6

        @pl.when((last >= 0) & (last < NB - 4) & (last % 4 == 3))
        def _():
            for i in range(4):
                sibling_done(last - i)
            weight_grads([blocks(xall, full, last - 3, 4), blocks(xsib, fsib, last - 3, 4)])

    sibling_done(NB - 4)
    sibling_done(NB - 3)
    weight_grads([blocks(xall, full, NB - 4, 2), blocks(xsib, fsib, NB - 4, 2)])
    sibling_done(NB - 2)
    weight_grads([blocks(xall, full, NB - 2, 1), blocks(xsib, fsib, NB - 2, 1)])
    acts_ready(NB - 1, full.at[NB - 1, far], rs.at[NB - 1, 4])
    sibling_done(NB - 1)
    weight_grads([blocks(xall, full, NB - 1, 1), blocks(xsib, fsib, NB - 1, 1)])

    def folded(values):
        rows = jnp.sum((values * values).reshape(-1, 8, values.shape[1]), axis=0)
        out = rows[:, 0:128]
        for i in range(1, values.shape[1] // 128):
            out += rows[:, 128 * i : 128 * (i + 1)]
        return out

    squares = jnp.zeros((8, 128), F32)
    stores = []
    for j in range(2):
        squares += folded(acc_in[j]) + folded(acc_out[j])
    sq[0] = squares

    for slot, where in group_two:
        put(sq.at[0], sqr1.at[slot], s_one, srs.at[0], where)
    for j in range(2):
        out_in[j] = acc_in[j].astype(BF16)
        out_out[j] = acc_out[j].astype(BF16)
        stores.append(pltpu.make_async_copy(out_in.at[j], o_gin.at[:, j * Q : (j + 1) * Q], ls.at[j]))
        stores.append(pltpu.make_async_copy(out_out.at[j], o_gout.at[j * Q : (j + 1) * Q], ls.at[2 + j]))
    for store in stores:
        store.start()
    input_grad(jnp.int32(NB - 1))
    arrived(sqr1.at[1:16], srs.at[0])
    whole = sq[0] + jnp.sum(sqr1[1:16], axis=0)
    sq[1] = whole
    for slot, where in group_one:
        put(sq.at[1], sqr2.at[slot], s_two, srs.at[1], where)

    arrived(dxr.at[1:11], srs.at[2])
    total = dxs[0].astype(F32)
    for i in range(1, 11):
        total += dxr[i].astype(F32)
    o_dx[...] = total.astype(BF16)

    arrived(sqr2.at[1:16], srs.at[1])
    o_sum[...] = whole + jnp.sum(sqr2[1:16], axis=0)

    for store in stores:
        store.wait()
    split = sum(1 for b in range(SPLIT) if b % EVERY < OF)
    left(got, s_sum)
    left(got.at[0 : 96 - 2 * split], s_act)
    left(got.at[0 : 62 + 2 * split], s_pass)
    left(got.at[0:60], s_move)
    left(got.at[0:48], s_core)
    left(part, s_half)
    left(sqr1.at[1:16], s_one)
    left(sqr2.at[1:16], s_two)


def scale_kernel(squares, dx, gin, gout, o_dx, o_gin, o_gout):
    total = jnp.sum(squares[...], keepdims=True)
    factor = 1.0 / jnp.sqrt(total / (2.0 * D * FW) + 1e-06)
    o_dx[...] = dx[...]
    o_gin[...] = (gin[...].astype(F32) * factor).astype(BF16)
    o_gout[...] = (gout[...].astype(F32) * factor).astype(BF16)


def scaled(squares, in_grad, grad_in, grad_out):
    steps = 4
    fixed = lambda shape: pl.BlockSpec(shape, lambda i: (0, 0))
    moving = lambda: pl.BlockSpec((W // steps, W), lambda i: (i, 0))
    return pl.pallas_call(
        scale_kernel,
        grid=(steps,),
        out_shape=(
            jax.ShapeDtypeStruct((ROWS, W), BF16),
            jax.ShapeDtypeStruct((W, W), BF16),
            jax.ShapeDtypeStruct((W, W), BF16),
        ),
        in_specs=[fixed((8, 128)), fixed((ROWS, W)), moving(), moving()],
        out_specs=(fixed((ROWS, W)), moving(), moving()),
    )(squares, in_grad, grad_in, grad_out)


def shards(tokens, w_in, w_out, out_grad):
    vmem = pl.BlockSpec(memory_space=pltpu.VMEM)
    hbm = pl.BlockSpec(memory_space=pl.ANY)
    dma = pltpu.SemaphoreType.DMA
    in_grad, grad_in, grad_out, squares = pl.pallas_call(
        kernel,
        out_shape=(
            jax.ShapeDtypeStruct((ROWS, W), BF16),
            jax.ShapeDtypeStruct((W, W), BF16),
            jax.ShapeDtypeStruct((W, W), BF16),
            jax.ShapeDtypeStruct((8, 128), F32),
        ),
        in_specs=[hbm] * 4,
        out_specs=(vmem, hbm, hbm, vmem),
        scratch_shapes=[
            pltpu.VMEM((NB // 2, 2, 2, ROWS, W), BF16),
            pltpu.VMEM((NB // 2, 2, 2, ROWS, W), BF16),
            pltpu.VMEM((2, W, W), BF16),
            pltpu.VMEM((2, W, W), BF16),
            pltpu.VMEM((NB, 4, 2, ROWS, Q), BF16),
            pltpu.VMEM((NB * 6, ROWS, Q), BF16),
            pltpu.VMEM((NB, 2, ROWS, Q), BF16),
            pltpu.VMEM((NB, 4, 2, 2, HALF, Q), BF16),
            pltpu.VMEM((NB, 2, 2, 2, HALF, Q), BF16),
            pltpu.VMEM((2, W, Q), F32),
            pltpu.VMEM((2, Q, W), F32),
            pltpu.VMEM((2, W, Q), BF16),
            pltpu.VMEM((2, Q, W), BF16),
            pltpu.VMEM((NB, ROWS, W), BF16),
            pltpu.VMEM((16, ROWS, W), BF16),
            pltpu.VMEM((2, 8, 128), F32),
            pltpu.VMEM((16, 8, 128), F32),
            pltpu.VMEM((16, 8, 128), F32),
            dma((4,)),
            dma((8,)),
            dma((NB // 2, 2)),
            dma((NB, 7)),
            dma((2,)),
            dma((3,)),
            dma((5,)),
        ],
        compiler_params=pltpu.CompilerParams(
            collective_id=0, has_side_effects=True, vmem_limit_bytes=60 * 2**20
        ),
        cost_estimate=pl.CostEstimate(
            flops=12_100_000_000, bytes_accessed=10_000_000, transcendentals=400_000
        ),
    )(tokens, w_in, w_out, out_grad)
    return scaled(squares, in_grad, grad_in, grad_out)


def solution(mesh):
    placed = (
        P(("gy", "gx"), "gz"),
        P("gz", ("gx", "gy")),
        P(("gx", "gy"), "gz"),
        P(("gy", "gx"), "gz"),
    )
    return jax.shard_map(
        shards,
        mesh=mesh,
        in_specs=placed,
        out_specs=(P(("gy", "gx"), "gz"), P("gz", ("gx", "gy")), P(("gx", "gy"), "gz")),
        check_vma=False,
    )
```

time: 136 us -> 135 us (level)
  no operation moved by 1% of the time
where the time goes in v3:
time: 135 us
  Pallas kernels  134 us (99%)
    pallas_call x1, Pallas kernels, shards(): pl.pallas_call(kernel, out_shape=(jax.ShapeDtypeStruct((ROWS, W), BF16),...  130 us
    pallas_call x1, Pallas kernels, scaled(): pl.pallas_call(scale_kernel, grid=(steps,), out_shape=(jax.ShapeDtypeStru...  4.21 us

profile of v3, /device:TPU:1, one launch (start us, length us, event | category | flops | bytes accessed | tf_op | source)
XLA Modules:
  0.0 134.8 jit_solution(12133493107593193954)
XLA Ops:
  0.6 129.9 %shard_map.67 = (bf16[64,768]{1,0:T(8,128)(2,1)}, bf16[768,768]{1,0:T(8,128)(2,1)}, bf16[768,768]{1,0:T(8,128)(2,1)}, f32[8,128]{1,0:T(8,128)}) custom-call(bf16[64,768]{1,0:T(8,128)(2,1)} %tok.1, bf16[768,768]{1,0:T(8,128)(2,1)} %win.1, bf16[768,768]{1,0:T(8,128)(2,1)} %wout.1, bf16[64,768]{1,0:T(8,128)(2,1)} %dy.1), custom_call_target="tpu_custom_call" | custom-call | flops 12099999744 | bytes 10000000 | tf_op jit(solution)/shard_map/pallas_call | solution.py:446
  130.6 4.2 %shard_map.68 = (bf16[64,768]{1,0:T(8,128)(2,1)}, bf16[768,768]{1,0:T(8,128)(2,1)}, bf16[768,768]{1,0:T(8,128)(2,1)}) custom-call(f32[8,128]{1,0:T(8,128)} %get-tuple-element.7.squares, bf16[64,768]{1,0:T(8,128)(2,1)} %get-tuple-element.8.dx, bf16[768,768]{1,0:T(8,128)(2,1)} %get-tuple-element.9.gin, bf16[768,768]{1,0:T(8,128)(2,1)} %get-tuple-element.10.gout), custom_call_target="tpu_custom_call" | custom-call | tf_op jit(solution)/shard_map/pallas_call | solution.py:429

commit v4 on v3

--- a/solution.py
+++ b/solution.py
@@ -423,7 +423,7 @@
 
 
 def scaled(squares, in_grad, grad_in, grad_out):
-    steps = 4
+    steps = 2
     fixed = lambda shape: pl.BlockSpec(shape, lambda i: (0, 0))
     moving = lambda: pl.BlockSpec((W // steps, W), lambda i: (i, 0))
     return pl.pallas_call(

time: 135 us -> 134 us (level)
  no operation moved by 1% of the time
where the time goes in v4:
time: 134 us
  Pallas kernels  133 us (99%)
    pallas_call x1, Pallas kernels, shards(): pl.pallas_call(kernel, out_shape=(jax.ShapeDtypeStruct((ROWS, W), BF16),...  130 us
    pallas_call x1, Pallas kernels, scaled(): pl.pallas_call(scale_kernel, grid=(steps,), out_shape=(jax.ShapeDtypeStru...  3.09 us

profile of v4, /device:TPU:1, one launch (start us, length us, event | category | flops | bytes accessed | tf_op | source)
XLA Modules:
  0.0 133.7 jit_solution(17594721123871541736)
XLA Ops:
  0.6 129.9 %shard_map.67 = (bf16[64,768]{1,0:T(8,128)(2,1)}, bf16[768,768]{1,0:T(8,128)(2,1)}, bf16[768,768]{1,0:T(8,128)(2,1)}, f32[8,128]{1,0:T(8,128)}) custom-call(bf16[64,768]{1,0:T(8,128)(2,1)} %tok.1, bf16[768,768]{1,0:T(8,128)(2,1)} %win.1, bf16[768,768]{1,0:T(8,128)(2,1)} %wout.1, bf16[64,768]{1,0:T(8,128)(2,1)} %dy.1), custom_call_target="tpu_custom_call" | custom-call | flops 12099999744 | bytes 10000000 | tf_op jit(solution)/shard_map/pallas_call | solution.py:446
  130.6 3.1 %shard_map.68 = (bf16[64,768]{1,0:T(8,128)(2,1)}, bf16[768,768]{1,0:T(8,128)(2,1)}, bf16[768,768]{1,0:T(8,128)(2,1)}) custom-call(f32[8,128]{1,0:T(8,128)} %get-tuple-element.7.squares, bf16[64,768]{1,0:T(8,128)(2,1)} %get-tuple-element.8.dx, bf16[768,768]{1,0:T(8,128)(2,1)} %get-tuple-element.9.gin, bf16[768,768]{1,0:T(8,128)(2,1)} %get-tuple-element.10.gout), custom_call_target="tpu_custom_call" | custom-call | tf_op jit(solution)/shard_map/pallas_call | solution.py:429

commit v5 on v4

--- a/solution.py
+++ b/solution.py
@@ -106,8 +106,8 @@
     put(xall.at[0, 0], xall.at[1, 0], s_move, xr.at[1, 0], z_up)
     put(xall.at[0, 0], xall.at[1, 1], s_move, xr.at[1, 1], z_down)
     loads[2].wait()
+    put(wown.at[0], wsib.at[0], s_core, wrs.at[0], to_sib)
     loads[3].wait()
-    put(wown.at[0], wsib.at[0], s_core, wrs.at[0], to_sib)
     put(wown.at[1], wsib.at[1], s_core, wrs.at[1], to_sib)
 
     def one(b, x, g, which, w_in, w_out):
@@ -124,12 +124,15 @@
         put(part.at[b, up, 1], got.at[6 * b + 2], s_sum, rs.at[b, 1], to_up)
         put(part.at[b, down, 0], got.at[6 * b + 3], s_sum, rs.at[b, 1], to_down)
 
-    put(xall.at[0, 0], xsib.at[0, 0], s_half, rs.at[0, 6], to_sib)
     one(0, xall[0, 0, 0], xall[0, 0, 1], 0, wown[0], wown[1])
     arrived(wsib.at[0], wrs.at[0])
+    h = contract(xall[0, 0, 0], wsib[0], 1, 0).astype(BF16)
+    part[0, 2, 0], part[0, 3, 0] = h[:, :Q], h[:, Q:]
     arrived(wsib.at[1], wrs.at[1])
-    one(0, xall[0, 0, 0], xall[0, 0, 1], 1, wsib[0], wsib[1])
+    d = contract(xall[0, 0, 1], wsib[1], 1, 1).astype(BF16)
+    part[0, 2, 1], part[0, 3, 1] = d[:, :Q], d[:, Q:]
     send_products(0)
+    put(xall.at[0, 0], xsib.at[0, 0], s_half, rs.at[0, 6], to_sib)
 
     def products(b):
         slot, side = b // 2, b % 2

time: 134 us -> 134 us (level)
  no operation moved by 1% of the time
where the time goes in v5:
time: 134 us
  Pallas kernels  133 us (99%)
    pallas_call x1, Pallas kernels, shards(): pl.pallas_call(kernel, out_shape=(jax.ShapeDtypeStruct((ROWS, W), BF16),...  130 us
    pallas_call x1, Pallas kernels, scaled(): pl.pallas_call(scale_kernel, grid=(steps,), out_shape=(jax.ShapeDtypeStru...  3.09 us

profile of v5, /device:TPU:1, one launch (start us, length us, event | category | flops | bytes accessed | tf_op | source)
XLA Modules:
  0.0 133.6 jit_solution(10363937325887865607)
XLA Ops:
  0.6 129.8 %shard_map.67 = (bf16[64,768]{1,0:T(8,128)(2,1)}, bf16[768,768]{1,0:T(8,128)(2,1)}, bf16[768,768]{1,0:T(8,128)(2,1)}, f32[8,128]{1,0:T(8,128)}) custom-call(bf16[64,768]{1,0:T(8,128)(2,1)} %tok.1, bf16[768,768]{1,0:T(8,128)(2,1)} %win.1, bf16[768,768]{1,0:T(8,128)(2,1)} %wout.1, bf16[64,768]{1,0:T(8,128)(2,1)} %dy.1), custom_call_target="tpu_custom_call" | custom-call | flops 12099999744 | bytes 10000000 | tf_op jit(solution)/shard_map/pallas_call | solution.py:449
  130.5 3.1 %shard_map.68 = (bf16[64,768]{1,0:T(8,128)(2,1)}, bf16[768,768]{1,0:T(8,128)(2,1)}, bf16[768,768]{1,0:T(8,128)(2,1)}) custom-call(f32[8,128]{1,0:T(8,128)} %get-tuple-element.7.squares, bf16[64,768]{1,0:T(8,128)(2,1)} %get-tuple-element.8.dx, bf16[768,768]{1,0:T(8,128)(2,1)} %get-tuple-element.9.gin, bf16[768,768]{1,0:T(8,128)(2,1)} %get-tuple-element.10.gout), custom_call_target="tpu_custom_call" | custom-call | tf_op jit(solution)/shard_map/pallas_call | solution.py:432
